TPU v7x, 128 devices: a whole 4x4x4 slice. The times are simulated.
128 devices in a mesh: member: 16 (over y_hi, x, core), grid: 8 (over z, y_lo).
Axes of the slice: x: 4, y: 4 (y_hi: 2, y_lo: 2; y = y_hi * 2 + y_lo), z: 4, core: 2. Of those that a mesh axis runs over, the one named last changes fastest.
Arguments:
- alpha_field: bfloat16 [16, 16, 512, 1024], P('member', None, 'grid'), may hold values from -6 to 6
- perturbation: bfloat16 [16, 2, 16, 512, 1024], P('member', None, None, 'grid'), may hold values from -1.5 to 1.5
- innovation: bfloat16 [2, 16, 512, 1024], P(None, None, 'grid'), may hold values from -6 to 6
- obs_weight: float32 [2, 16, 512], P(None, None, 'grid'), may hold values from 0.5 to 2
- row_class: int32 [16, 512], P(None, 'grid'), may hold values from 0 to 2
- column_class: int32 [16, 1024], P(None, 'grid'), may hold values from 0 to 2
- row_factor: bfloat16 [3, 1024, 1024], replicated, may hold values from 0 to 2, as said below
- column_factor: bfloat16 [3, 512, 512], replicated, may hold values from 0 to 2, as said below
- level_factor: bfloat16 [16, 16], replicated, may hold values from 0 to 2, as said below
Outputs:
- gradient: bfloat16 [16, 16, 512, 1024], P('member', None, 'grid')
- increment: bfloat16 [2, 16, 512, 1024], P(None, None, 'grid')
Inputs may be any that keep to these rules, and one draw needn't show every extreme that they name: `row_factor`: zero below the diagonal. `column_factor`: zero below the diagonal. `level_factor`: zero below the diagonal.
All inputs are finite; a program needn't handle non-finite values.
Results may differ from a plain program's by a relative error of at most 0.023.
Values may be sent and summed in bfloat16 or wider, within the bound.
A program may use at most 128 MiB of HBM per device.

v0:
```python
import functools

import jax
import jax.numpy as jnp
from jax import lax
from jax.experimental import pallas as pl
from jax.experimental.pallas import tpu as pltpu
from jax.sharding import PartitionSpec as P

MESH = pl.DeviceIdType.MESH
F32 = jnp.float32
BF16 = jnp.bfloat16

CLASSES = 3
LEVELS = 16
GROUP = 8
RING = 4
CHUNKS = 4
PART = LEVELS // CHUNKS
ROWS = 64
ROW_BITS = 6
LANES = 128
NX = GROUP * LANES
NY = GROUP * ROWS
LINES = PART * ROWS
PAIR = 2
TILE = 256
TILES = NX // TILE
WIDE = 2
DEEP = TILE // ROWS


def loop(count, body):
    def step(index, carry):
        body(index)
        return carry

    lax.fori_loop(0, count, step, 0)


def dot(a, b):
    return jnp.dot(a, b, preferred_element_type=F32)


def dot_nt(a, b):
    return lax.dot_general(a, b, (((1,), (1,)), ((), ())), preferred_element_type=F32)


def kernel(
    alpha_h, pert_h, innov_h, weight_ref, row_ref, col_ref, rowf_h, colf_h, level_ref,
    grad_h, inc_h,
    alpha_v, pert_v, innov_v, rowf, colf, colt, down, back, row_hot, col_hot, weight_v, masked,
    slabs, lines, filtered, turned, local_s, local_r, core_s, core_r, x_in, x_got, y_s, y_r,
    inc, inc_v,
    alpha_sem, rowf_sem, load_sem, grad_sem, inc_sem, out_sem, a2a_ss, a2a_rs, core_ss, core_rs,
    x_ss, xin_rs, xgot_rs, yr_ss, yr_rs, give_ss, xa_rs, xf_rs, ca_rs,
):
    m = lax.axis_index("member")
    g = lax.axis_index("grid")
    y_hi = m // (2 * RING)
    x = lax.rem(m // 2, RING)
    core = lax.rem(m, 2)
    sibling = m + 1 - 2 * core
    across = m + 2 * RING - 4 * RING * y_hi

    def around(position, way, steps=1):
        return lax.rem(position + (steps if way == 0 else RING - steps), RING)

    def x_peer(way):
        return y_hi * (2 * RING) + around(x, way) * 2 + core

    def lane(s):
        return pl.ds(pl.multiple_of(s * LANES, LANES), LANES)

    def slab_rows(s):
        return pl.ds(pl.multiple_of(s * ROWS, ROWS), ROWS)

    def part(c):
        return pl.ds(c * PART, PART)

    barrier = pltpu.get_barrier_semaphore()

    def greet(partner):
        pl.semaphore_signal(barrier, inc=1, device_id=partner, device_id_type=MESH)

    loop(GROUP - 1, lambda step: greet((m, lax.rem(g + step + 1, GROUP))))
    for member in (x_peer(0), x_peer(1), sibling, across):
        greet((member, g))

    def alpha_load(c):
        return pltpu.make_async_copy(alpha_h.at[part(c)], alpha_v.at[part(c)], alpha_sem.at[c])

    def rowf_load(n):
        depth = (n // WIDE + 1) * WIDE * TILE
        where = (slice(None), slice(0, depth), slice(n * TILE, (n + 1) * TILE))
        return pltpu.make_async_copy(rowf_h.at[where], rowf.at[where], rowf_sem.at[n])

    alpha_load(0).start()
    for n in range(NX // TILE):
        rowf_load(n).start()
    loads = [
        pltpu.make_async_copy(src, dst, load_sem.at[i])
        for i, (src, dst) in enumerate(((colf_h, colf), (pert_h, pert_v), (innov_h, innov_v)))
    ]

    diagonal = lax.broadcasted_iota(jnp.int32, (ROWS, ROWS), 0) == lax.broadcasted_iota(
        jnp.int32, (ROWS, ROWS), 1
    )

    def upright(line):
        spread = jnp.where(diagonal, jnp.broadcast_to(line, (ROWS, ROWS)), 0.0)
        return jnp.broadcast_to(jnp.sum(spread, axis=1, keepdims=True), (ROWS, LANES))

    def row_table(z):
        column = upright(row_ref[pl.ds(z, 1), :].astype(F32))
        for c in range(CLASSES):
            row_hot[c, slab_rows(z), :] = jnp.where(column == c, 1.0, 0.0).astype(BF16)

    def tile_span(n):
        return slice(n * TILE, (n + 1) * TILE)

    def iota(shape, axis):
        return lax.broadcasted_iota(jnp.int32, shape, axis)

    def level_table(table, product):
        wide = (LEVELS, LEVELS * ROWS)
        spread = jnp.where(iota(wide, 0) == iota(wide, 1) >> ROW_BITS, 1.0, 0.0).astype(BF16)
        tall = (TILE, LEVELS * ROWS)
        same = (iota(tall, 0) & (ROWS - 1)) == (iota(tall, 1) & (ROWS - 1))
        level = level_ref[...]
        for b in range(LEVELS * ROWS // TILE):
            short = (TILE, LEVELS)
            spot = (iota(short, 0) >> ROW_BITS) + b * DEEP
            pick = jnp.where(spot == iota(short, 1), 1.0, 0.0).astype(BF16)
            table[b * TILE : (b + 1) * TILE, :] = jnp.where(
                same, dot(product(pick, level).astype(BF16), spread), 0.0
            ).astype(BF16)

    def column_tables():
        def column_table(z):
            line = jnp.broadcast_to(col_ref[pl.ds(z, 1), :], (16, LANES))
            for c in range(CLASSES):
                col_hot[c, z] = jnp.where(line == c, 1.0, 0.0).astype(BF16)

        loop(LEVELS, column_table)
        level_table(down, dot_nt)
        loads[0].wait()
        unit = jnp.where(iota((NY, NY), 0) == iota((NY, NY), 1), 1.0, 0.0).astype(BF16)

        def turn(c):
            colt[c] = dot_nt(unit, colf[c]).astype(BF16)

        loop(CLASSES, turn)

    def turn_rows(k):
        unit = jnp.where(iota((TILE, TILE), 0) == iota((TILE, TILE), 1), 1.0, 0.0).astype(BF16)
        for r in range(TILES):
            for d in range(r, TILES):
                rowf[k, tile_span(d), tile_span(r)] = dot_nt(
                    unit, rowf[k, tile_span(r), tile_span(d)]
                ).astype(BF16)

    def adjoint_tables():
        def weight_table(z):
            for t in range(2):
                weight_v[t, z] = upright(weight_ref[t, pl.ds(z, 1), :]).astype(BF16)

        loop(LEVELS, weight_table)
        level_table(back, dot)

    def remote(src, dst, ss, rs, member, group):
        return pltpu.make_async_remote_copy(
            src_ref=src, dst_ref=dst, send_sem=ss, recv_sem=rs,
            device_id=(member, group), device_id_type=MESH,
        )

    z_at = g // 2
    y_lo = lax.rem(g, 2)

    def send(phase, c, src, dst, peer):
        remote(src(peer), dst(g), a2a_ss.at[phase], a2a_rs.at[phase, c], m, peer).start()

    def exchange(phase, c, src, dst):
        for up, side in ((2, 0), (1, 0), (3, 0), (2, 1), (1, 1), (3, 1), (0, 1)):
            y_peer = y_lo if side == 0 else 1 - y_lo
            send(phase, c, src, dst, lax.rem(z_at + up, RING) * 2 + y_peer)

    def came(sem, view):
        remote(view, view, out_sem, sem, sibling, g).wait_recv()

    def left(sem, view):
        remote(view, view, sem, out_sem, sibling, g).wait_send()

    def lines_came(phase, c):
        came(a2a_rs.at[phase, c], lines.at[c, pl.ds(0, GROUP - 1)])

    def local_came(phase, c):
        came(a2a_rs.at[phase, c], local_r.at[c, pl.ds(0, GROUP - 1)])

    def exchange_left(phase):
        left(a2a_ss.at[phase], lines.at[:, pl.ds(0, GROUP - 1)])

    def line_block(c):
        return lambda s: lines.at[c, s]

    def filtered_block(c):
        return lambda s: filtered.at[c, s]

    def weighted_block(c):
        return lambda s: core_s.at[c, s]

    def slab_block(c):
        return lambda s: slabs.at[c, s]

    def local_block(c):
        return lambda s: local_r.at[c, s]

    def own_block(c):
        return lambda s: local_s.at[c, s]

    def mask_lines(c, source):
        span = pl.ds(pl.multiple_of(c * LINES, LINES), PAIR * LINES)
        hots = [row_hot[k, span, :] for k in range(CLASSES)]
        for n in range(TILES):
            tile = source(n)
            for k in range(CLASSES):
                at_lane = (n * CLASSES + k) * TILE
                masked[:, at_lane : at_lane + TILE] = tile * jnp.concatenate([hots[k]] * 2, axis=1)

    def levels(c):
        return pl.ds(c * PART, PAIR * PART)

    def row_filter(c):
        @pl.when(lax.rem(c, PAIR) == 0)
        def _():
            filter_rows(c)

        lines[c, g] = slabs[c, g]

        @pl.when(c > 0)
        def _():
            exchange(0, c, slab_block(c), line_block(c))

        @pl.when(c == 0)
        def _():
            for load in loads:
                load.start()

    def filter_rows(c):
        for j in range(PAIR):
            alpha_load(c + j).wait()
        loop(PAIR * PART, lambda z: row_table(c * PART + z))
        mask_lines(c, lambda n: alpha_v[levels(c), :, tile_span(n)].reshape(PAIR * LINES, TILE))
        for first in range(0, TILES, WIDE):
            last = first + WIDE

            @pl.when(c == 0)
            def _():
                for n in range(first, last):
                    rowf_load(n).wait()

            table = jnp.concatenate(
                [
                    rowf[k, tile_span(d), first * TILE : last * TILE]
                    for d in range(last)
                    for k in range(CLASSES)
                ],
                axis=0,
            )
            total = dot(masked[:, : last * CLASSES * TILE], table).astype(BF16)
            for j in range(2 * WIDE):
                s = 2 * first + j
                slabs[pl.ds(c, PAIR), s] = total[:, j * LANES : (j + 1) * LANES].reshape(
                    PAIR, PART, ROWS, LANES
                )

                @pl.when(jnp.logical_and(c == 0, g != s))
                def _():
                    send(0, c, slab_block(c), line_block(c), s)

    def column_pass(c, source, table, upper):
        whole = jnp.concatenate(
            [source[c, :, j].reshape(NY, LANES) for j in range(PART)], axis=1
        )
        blocks = []
        for k in range(CLASSES):
            hot = jnp.concatenate([col_hot[k, c * PART + j] for j in range(PART)], axis=1)
            blocks.append(
                (whole.reshape(NY // 16, 16, PART * LANES) * hot[None]).reshape(NY, PART * LANES)
            )
        half = NY // 2
        low = slice(0, half)
        high = slice(half, NY)

        def product(out, deep):
            return dot(
                jnp.concatenate([table[k, out, deep] for k in range(CLASSES)], axis=1),
                jnp.concatenate([block[deep] for block in blocks], axis=0),
            )

        first = product(low, slice(0, NY) if upper else low)
        second = product(high, high if upper else slice(0, NY))
        for j in range(PART):
            side = slice(j * LANES, (j + 1) * LANES)
            for n, total in enumerate((first, second)):
                filtered[c, n * GROUP // 2 : (n + 1) * GROUP // 2, j] = (
                    total[:, side].astype(BF16).reshape(GROUP // 2, ROWS, LANES)
                )

    def level_pass(c, table, source, target, deep):
        for chunk in range(CHUNKS):

            @pl.when(c == chunk)
            def _(chunks=deep(chunk), rows=slice(chunk * LINES, (chunk + 1) * LINES)):
                held = slice(chunks[0], chunks[-1] + 1)
                span = slice(chunks[0] * LINES, (chunks[-1] + 1) * LINES)

                def some(i):
                    block = jnp.concatenate(
                        [source[held, 4 * i + j].reshape(-1, LANES) for j in range(4)], axis=1
                    )
                    total = dot(table[rows, span], block).astype(BF16)
                    for j in range(4):
                        target(
                            4 * i + j,
                            total[:, j * LANES : (j + 1) * LANES].reshape(PART, ROWS, LANES),
                        )

                loop(GROUP // 4, some)

    def column_filter(c):
        lines_came(0, c)
        column_pass(c, lines, colt, False)

        def keep(s, block):
            local_s[c, s] = block

        level_pass(c, down, filtered, keep, lambda chunk: range(chunk + 1))
        local_r[c, g] = local_s[c, g]
        exchange(1, c, own_block(c), local_block(c))

    def core_copy(c):
        return pltpu.make_async_remote_copy(
            src_ref=core_s.at[c],
            dst_ref=core_r.at[c],
            send_sem=core_ss.at[c],
            recv_sem=core_rs.at[c],
            device_id=(sibling, g),
            device_id_type=MESH,
        )

    def xin_slab(way):
        return 2 * around(x, way, 2) + way

    def xone_slab(way):
        return 2 * around(x, way) + 1 - way

    def xtwo_slab(way):
        return 2 * around(x, way) + way

    def x_copy(src, dst, sem, way):
        return remote(src, dst, x_ss, sem, x_peer(way), g)

    def y_copy(c):
        return pltpu.make_async_remote_copy(
            src_ref=y_s.at[c],
            dst_ref=y_r.at[c],
            send_sem=yr_ss,
            recv_sem=yr_rs.at[c],
            device_id=(across, g),
            device_id_type=MESH,
        )

    def term(t, c, s):
        return pert_v[t, part(c), :, lane(s)] * local_r[c, s]

    def sum_core(c):
        local_came(1, c)

        @pl.when(c == 0)
        def _():
            loads[1].wait()
            loads[2].wait()

        def one(s):
            core_s[c, s] = term(1 - core, c, s)

        loop(GROUP, one)
        core_copy(c).start()

    def sum_x(c):
        core_copy(c).wait_recv()

        def add(s):
            core_r[c, s] = term(core, c, s) + core_r[c, s]

        for way in range(2):
            s = xin_slab(way)
            add(s)
            x_copy(core_r.at[c, s], x_in.at[c, way], xin_rs.at[c], way).start()
        for way in range(2):
            s = xone_slab(way)
            add(s)
            x_copy(core_r.at[c, s], x_got.at[c, 0, way], xgot_rs.at[c], way).start()
        for way in range(2):
            add(xtwo_slab(way))
        for j in range(2):
            add(2 * x + j)

    def add_x(c):
        came(xin_rs.at[c], x_in.at[c])
        for way in range(2):
            slab = xtwo_slab(way)
            x_in[c, way] = x_in[c, way] + core_r[c, slab]
            x_copy(x_in.at[c, way], x_got.at[c, 1, way], xgot_rs.at[c], way).start()

    def sum_y(c):
        came(xgot_rs.at[c], x_got.at[c])
        for j in range(2):
            total = core_r[c, 2 * x + j].astype(F32) + x_got[c, 1, j].astype(F32)
            y_s[c, j] = (total + x_got[c, 0, 1 - j].astype(F32)).astype(BF16)
        y_copy(c).start()

    def give(rs, t, c, s, member):
        return remote(inc.at[t, c, s], inc.at[t, c, s], give_ss, rs, member, g)

    def finish(c):
        y_copy(c).wait_recv()
        for j in range(2):
            total = y_s[c, j].astype(F32) + y_r[c, j].astype(F32)
            inc[core, c, 2 * x + j] = total.astype(BF16)
        pair = inc.at[core, c, pl.ds(2 * x, 2)]
        for way in range(2):
            remote(pair, pair, give_ss, xa_rs.at[c], x_peer(way), g).start()

    def gather_x(c):
        came(xa_rs.at[c], inc.at[core, c, pl.ds(0, 4)])
        for way in range(2):
            slab = 2 * around(x, 1 - way) + way
            give(xf_rs.at[c], core, c, slab, x_peer(way)).start()

    def gather_far(c):
        came(xf_rs.at[c], inc.at[core, c, pl.ds(0, 2)])
        remote(inc.at[core, c], inc.at[core, c], give_ss, ca_rs.at[c], sibling, g).start()

    def weigh(c):
        def one(s):
            total = None
            for t in range(2):
                block = inc[t, c, s]
                inc_v[t, part(c), :, lane(s)] = block
                misfit = weight_v[t, part(c)] * (block - innov_v[t, part(c), :, lane(s)])
                share = pert_v[t, part(c), :, lane(s)] * misfit
                total = share if total is None else total + share
            core_s[c, s] = total

        core_copy(c).wait_send()
        came(ca_rs.at[c], inc.at[1 - core, c])
        loop(GROUP, one)
        lines[c, g] = core_s[c, g]
        exchange(2, c, weighted_block(c), line_block(c))
        inc_copy(c).start()

    def inc_copy(c):
        return pltpu.make_async_copy(
            inc_v.at[:, part(c)], inc_h.at[:, part(c)], inc_sem.at[c]
        )

    def column_adjoint(c):
        lines_came(2, c)

        def keep(s, block):
            turned[c, s] = block

        level_pass(c, back, lines, keep, lambda chunk: range(chunk, CHUNKS))
        column_pass(c, turned, colf, True)
        local_r[c, g] = filtered[c, g]
        exchange(3, c, filtered_block(c), local_block(c))

    def grad_copy(c):
        return pltpu.make_async_copy(alpha_v.at[part(c)], grad_h.at[part(c)], grad_sem.at[c])

    def row_adjoint(c):
        local_came(3, c)

        @pl.when(lax.rem(c, PAIR) == 0)
        def _():
            adjoin_rows(c)

    def adjoin_rows(c):
        mask_lines(
            c,
            lambda n: jnp.concatenate(
                [
                    local_r[pl.ds(c, PAIR), 2 * n + j].reshape(PAIR * LINES, LANES)
                    for j in range(2)
                ],
                axis=1,
            ),
        )
        for n in range(TILES):
            side = tile_span(n)
            table = jnp.concatenate(
                [rowf[k, tile_span(d), side] for d in range(n, TILES) for k in range(CLASSES)],
                axis=0,
            )
            total = dot(masked[:, n * CLASSES * TILE :], table)
            alpha = alpha_v[levels(c), :, side].reshape(PAIR * LINES, TILE).astype(F32)
            alpha_v[levels(c), :, side] = (
                (alpha + total).astype(BF16).reshape(PAIR * PART, ROWS, TILE)
            )
        for j in range(PAIR):
            grad_copy(c + j).start()

    pl.semaphore_wait(barrier, GROUP + 3)
    for c in range(1, CHUNKS):
        alpha_load(c).start()

    def at(step, offset, stage):
        chunk = step - offset

        @pl.when(jnp.logical_and(chunk >= 0, chunk < CHUNKS))
        def _():
            stage(chunk)

    def forward(step):
        @pl.when(jnp.logical_and(step >= CHUNKS + 1, step < CHUNKS + 1 + CLASSES))
        def _():
            turn_rows(step - CHUNKS - 1)

        @pl.when(step == 4)
        def _():
            adjoint_tables()

        at(step, 4, sum_core)
        at(step, 6, finish)
        at(step, 7, gather_far)
        at(step, 5, sum_y)
        at(step, 1, row_filter)
        at(step, 4, sum_x)
        at(step, 7, weigh)

        @pl.when(step == 2)
        def _():
            column_tables()

        at(step, 2, column_filter)
        at(step, 6, gather_x)
        at(step, 4, add_x)

    loop(CHUNKS + 7, forward)

    def backward(step):
        at(step, 0, lambda c: column_adjoint(CHUNKS - 1 - c))
        at(step, 2, lambda c: row_adjoint(CHUNKS - 1 - c))

    loop(CHUNKS + 2, backward)

    for phase in range(4):
        exchange_left(phase)
    left(x_ss, core_r.at[pl.ds(0, 3)])
    left(yr_ss, y_s)
    left(give_ss, pert_v.at[:, pl.ds(0, LEVELS - 2)])
    for c in range(CHUNKS):
        inc_copy(c).wait()
        grad_copy(c).wait()


def on_device(alpha, pert, innov, weight, row_class, col_class, rowf, colf, level):
    any_spec = pl.BlockSpec(memory_space=pl.ANY)
    vmem_spec = pl.BlockSpec(memory_space=pltpu.VMEM)
    dma = pltpu.SemaphoreType.DMA
    block = (PART, ROWS, LANES)
    slab = (CHUNKS, GROUP) + block
    scratch = [
        pltpu.VMEM((LEVELS, ROWS, NX), BF16),
        pltpu.VMEM((2, LEVELS, ROWS, NX), BF16),
        pltpu.VMEM((2, LEVELS, ROWS, NX), BF16),
        pltpu.VMEM((CLASSES, NX, NX), BF16),
        pltpu.VMEM((CLASSES, NY, NY), BF16),
        pltpu.VMEM((CLASSES, NY, NY), BF16),
        pltpu.VMEM((LEVELS * ROWS, LEVELS * ROWS), BF16),
        pltpu.VMEM((LEVELS * ROWS, LEVELS * ROWS), BF16),
        pltpu.VMEM((CLASSES, LEVELS * ROWS, LANES), BF16),
        pltpu.VMEM((CLASSES, LEVELS, 16, LANES), BF16),
        pltpu.VMEM((2, LEVELS, ROWS, LANES), BF16),
        pltpu.VMEM((PAIR * LINES, CLASSES * NX), BF16),
        pltpu.VMEM(slab, BF16),
        pltpu.VMEM(slab, BF16),
        pltpu.VMEM(slab, BF16),
        pltpu.VMEM(slab, BF16),
        pltpu.VMEM(slab, BF16),
        pltpu.VMEM(slab, BF16),
        pltpu.VMEM(slab, BF16),
        pltpu.VMEM(slab, BF16),
        pltpu.VMEM((CHUNKS, 2) + block, BF16),
        pltpu.VMEM((CHUNKS, 2, 2) + block, BF16),
        pltpu.VMEM((CHUNKS, 2) + block, BF16),
        pltpu.VMEM((CHUNKS, 2) + block, BF16),
        pltpu.VMEM((2,) + slab, BF16),
        pltpu.VMEM((2, LEVELS, ROWS, NX), BF16),
        dma((CHUNKS,)),
        dma((NX // TILE,)),
        dma((3,)),
        dma((CHUNKS,)),
        dma((CHUNKS,)),
        dma,
        dma((4,)),
        dma((4, CHUNKS)),
        dma((CHUNKS,)),
        dma((CHUNKS,)),
        dma,
        dma((CHUNKS,)),
        dma((CHUNKS,)),
        dma,
        dma((CHUNKS,)),
        dma,
        dma((CHUNKS,)),
        dma((CHUNKS,)),
        dma((CHUNKS,)),
    ]
    gradient, increment = pl.pallas_call(
        kernel,
        out_shape=(
            jax.ShapeDtypeStruct((LEVELS, ROWS, NX), BF16),
            jax.ShapeDtypeStruct((2, LEVELS, ROWS, NX), BF16),
        ),
        in_specs=[any_spec] * 3 + [vmem_spec] * 3 + [any_spec] * 2 + [vmem_spec],
        out_specs=(any_spec, any_spec),
        scratch_shapes=scratch,
        compiler_params=pltpu.CompilerParams(
            collective_id=0, has_side_effects=True, vmem_limit_bytes=62 * 1024 * 1024
        ),
    )(alpha[0], pert[0], innov, weight, row_class, col_class, rowf, colf, level)
    return gradient[None], increment


def solution(mesh):
    return jax.shard_map(
        on_device,
        mesh=mesh,
        in_specs=(
            P("member", None, "grid", None),
            P("member", None, None, "grid", None),
            P(None, None, "grid", None),
            P(None, None, "grid"),
            P(None, "grid"),
            P(None, "grid"),
            P(),
            P(),
            P(),
        ),
        out_specs=(P("member", None, "grid", None), P(None, None, "grid", None)),
        check_vma=False,
    )
```

profile of v0, /device:TPU:1, one launch (start us, length us, event | category | flops | bytes accessed | tf_op | source)
XLA Modules:
  0.0 139.0 jit_solution(11944526255787369607)
XLA Ops:
  0.6 133.0 %shard_map.104 = (bf16[16,64,1024]{2,1,0:T(8,128)(2,1)}, bf16[2,16,64,1024]{3,2,1,0:T(8,128)(2,1)}) custom-call(bf16[16,64,1024]{2,1,0:T(8,128)(2,1)} %bitcast.4, bf16[2,16,64,1024]{3,2,1,0:T(8,128)(2,1)} %bitcast.3, bf16[2,16,64,1024]{3,2,1,0:T(8,128)(2,1)} %innov_h.1, f32[2,16,64]{2,1,0:T(8,128)} %weight_ref.1, s32[16,64]{1,0:T(8,128)} %row_ref.1, ...), custom_call_target="tpu_custom_call" | custom-call | tf_op jit(solution)/shard_map/pallas_call | solution.py:622
  133.7 0.0 copy-start
  133.7 3.3 %copy.13 = bf16[1,16,64,1024]{3,2,1,0:T(8,128)(2,1)} copy(bf16[1,16,64,1024]{3,2,1,0:T(8,128)(2,1)} %bitcast.5) | data formatting | bytes 4194304
  137.0 0.0 copy-done
  137.0 2.0 %copy.14 = bf16[2,16,64,1024]{3,2,1,0:T(8,128)(2,1)} copy(bf16[2,16,64,1024]{3,2,1,0:T(8,128)(2,1)S(1)} %copy-done) | data formatting | bytes 8388608
Async XLA Ops:
  133.7 3.3 %copy-start = (bf16[2,16,64,1024]{3,2,1,0:T(8,128)(2,1)S(1)}, bf16[2,16,64,1024]{3,2,1,0:T(8,128)(2,1)}, u32[]{:S(2)}) copy-start(bf16[2,16,64,1024]{3,2,1,0:T(8,128)(2,1)} %get-tuple-element.9) | copy-start | bytes 12582916
where the time goes:
time: 139 us
  Pallas kernels  133 us (96%)
  local copies, waits for them, and re-layouts  5.31 us (4%)
    pallas_call x1, Pallas kernels, on_device(): pl.pallas_call(kernel, out_shape=(jax.ShapeDtypeStruct((LEVELS, ROWS, NX)...  133 us
    unnamed x4, local copies, waits for them, and re-layouts  5.31 us

commit v1 on v0

--- a/solution.py
+++ b/solution.py
@@ -49,7 +49,7 @@
 def kernel(
     alpha_h, pert_h, innov_h, weight_ref, row_ref, col_ref, rowf_h, colf_h, level_ref,
     grad_h, inc_h,
-    alpha_v, pert_v, innov_v, rowf, colf, colt, down, back, row_hot, col_hot, weight_v, masked,
+    alpha_v, pert_v, innov_v, rowf, colf, colt, down, back, row_hot, weight_v, masked,
     slabs, lines, filtered, turned, local_s, local_r, core_s, core_r, x_in, x_got, y_s, y_r,
     inc, inc_v,
     alpha_sem, rowf_sem, load_sem, grad_sem, inc_sem, out_sem, a2a_ss, a2a_rs, core_ss, core_rs,
@@ -137,12 +137,6 @@
             ).astype(BF16)
 
     def column_tables():
-        def column_table(z):
-            line = jnp.broadcast_to(col_ref[pl.ds(z, 1), :], (16, LANES))
-            for c in range(CLASSES):
-                col_hot[c, z] = jnp.where(line == c, 1.0, 0.0).astype(BF16)
-
-        loop(LEVELS, column_table)
         level_table(down, dot_nt)
         loads[0].wait()
         unit = jnp.where(iota((NY, NY), 0) == iota((NY, NY), 1), 1.0, 0.0).astype(BF16)
@@ -282,24 +276,30 @@
         whole = jnp.concatenate(
             [source[c, :, j].reshape(NY, LANES) for j in range(PART)], axis=1
         )
-        blocks = []
-        for k in range(CLASSES):
-            hot = jnp.concatenate([col_hot[k, c * PART + j] for j in range(PART)], axis=1)
-            blocks.append(
-                (whole.reshape(NY // 16, 16, PART * LANES) * hot[None]).reshape(NY, PART * LANES)
-            )
+        kind = jnp.concatenate([col_ref[pl.ds(c * PART + j, 1), :] for j in range(PART)], axis=1)
+        kind = jnp.broadcast_to(kind, (NY // 2, PART * LANES))
+
+        def pick(products):
+            return jnp.where(kind == 0, products[0], jnp.where(kind == 1, products[1], products[2]))
+
+        def product(rows, deep):
+            stacked = jnp.concatenate([table[k, rows, deep] for k in range(CLASSES)], axis=0)
+            total = dot(stacked, whole[deep])
+            count = total.shape[0] // CLASSES
+            return [total[k * count : (k + 1) * count] for k in range(CLASSES)]
+
         half = NY // 2
         low = slice(0, half)
         high = slice(half, NY)
-
-        def product(out, deep):
-            return dot(
-                jnp.concatenate([table[k, out, deep] for k in range(CLASSES)], axis=1),
-                jnp.concatenate([block[deep] for block in blocks], axis=0),
-            )
-
-        first = product(low, slice(0, NY) if upper else low)
-        second = product(high, high if upper else slice(0, NY))
+        both = slice(0, NY)
+        wide = product(both, high if upper else low)
+        narrow = product(low if upper else high, low if upper else high)
+        first = pick([block[low] for block in wide])
+        second = pick([block[high] for block in wide])
+        if upper:
+            first += pick(narrow)
+        else:
+            second += pick(narrow)
         for j in range(PART):
             side = slice(j * LANES, (j + 1) * LANES)
             for n, total in enumerate((first, second)):
@@ -582,7 +582,6 @@
         pltpu.VMEM((LEVELS * ROWS, LEVELS * ROWS), BF16),
         pltpu.VMEM((LEVELS * ROWS, LEVELS * ROWS), BF16),
         pltpu.VMEM((CLASSES, LEVELS * ROWS, LANES), BF16),
-        pltpu.VMEM((CLASSES, LEVELS, 16, LANES), BF16),
         pltpu.VMEM((2, LEVELS, ROWS, LANES), BF16),
         pltpu.VMEM((PAIR * LINES, CLASSES * NX), BF16),
         pltpu.VMEM(slab, BF16),

time: 139 us -> 139 us (level)
  no operation moved by 1% of the time
where the time goes in v1:
time: 139 us
  Pallas kernels  133 us (96%)
  local copies, waits for them, and re-layouts  5.31 us (4%)
    pallas_call x1, Pallas kernels, on_device(): pl.pallas_call(kernel, out_shape=(jax.ShapeDtypeStruct((LEVELS, ROWS, NX)...  133 us
    unnamed x4, local copies, waits for them, and re-layouts  5.31 us

profile of v1, /device:TPU:1, one launch (start us, length us, event | category | flops | bytes accessed | tf_op | source)
XLA Modules:
  0.0 139.0 jit_solution(15536765633826413527)
XLA Ops:
  0.6 133.0 %shard_map.104 = (bf16[16,64,1024]{2,1,0:T(8,128)(2,1)}, bf16[2,16,64,1024]{3,2,1,0:T(8,128)(2,1)}) custom-call(bf16[16,64,1024]{2,1,0:T(8,128)(2,1)} %bitcast.4, bf16[2,16,64,1024]{3,2,1,0:T(8,128)(2,1)} %bitcast.3, bf16[2,16,64,1024]{3,2,1,0:T(8,128)(2,1)} %innov_h.1, f32[2,16,64]{2,1,0:T(8,128)} %weight_ref.1, s32[16,64]{1,0:T(8,128)} %row_ref.1, ...), custom_call_target="tpu_custom_call" | custom-call | tf_op jit(solution)/shard_map/pallas_call | solution.py:621
  133.7 0.0 copy-start
  133.7 3.3 %copy.13 = bf16[1,16,64,1024]{3,2,1,0:T(8,128)(2,1)} copy(bf16[1,16,64,1024]{3,2,1,0:T(8,128)(2,1)} %bitcast.5) | data formatting | bytes 4194304
  137.0 0.0 copy-done
  137.0 2.0 %copy.14 = bf16[2,16,64,1024]{3,2,1,0:T(8,128)(2,1)} copy(bf16[2,16,64,1024]{3,2,1,0:T(8,128)(2,1)S(1)} %copy-done) | data formatting | bytes 8388608
Async XLA Ops:
  133.7 3.3 %copy-start = (bf16[2,16,64,1024]{3,2,1,0:T(8,128)(2,1)S(1)}, bf16[2,16,64,1024]{3,2,1,0:T(8,128)(2,1)}, u32[]{:S(2)}) copy-start(bf16[2,16,64,1024]{3,2,1,0:T(8,128)(2,1)} %get-tuple-element.9) | copy-start | bytes 12582916

commit v2 on v1

--- a/solution.py
+++ b/solution.py
@@ -16,6 +16,7 @@
 GROUP = 8
 RING = 4
 CHUNKS = 4
+PIECES = 4
 PART = LEVELS // CHUNKS
 ROWS = 64
 ROW_BITS = 6
@@ -174,10 +175,13 @@
     def send(phase, c, src, dst, peer):
         remote(src(peer), dst(g), a2a_ss.at[phase], a2a_rs.at[phase, c], m, peer).start()
 
+    def peers():
+        for up, side in ((2, 0), (1, 0), (3, 0), (2, 1), (1, 1), (3, 1), (0, 1)):
+            yield lax.rem(z_at + up, RING) * 2 + (y_lo if side == 0 else 1 - y_lo)
+
     def exchange(phase, c, src, dst):
-        for up, side in ((2, 0), (1, 0), (3, 0), (2, 1), (1, 1), (3, 1), (0, 1)):
-            y_peer = y_lo if side == 0 else 1 - y_lo
-            send(phase, c, src, dst, lax.rem(z_at + up, RING) * 2 + y_peer)
+        for peer in peers():
+            send(phase, c, src, dst, peer)
 
     def came(sem, view):
         remote(view, view, out_sem, sem, sibling, g).wait_recv()
@@ -335,18 +339,16 @@
         def keep(s, block):
             local_s[c, s] = block
 
+            @pl.when(s != g)
+            def _():
+                send(1, c, own_block(c), local_block(c), s)
+
         level_pass(c, down, filtered, keep, lambda chunk: range(chunk + 1))
         local_r[c, g] = local_s[c, g]
-        exchange(1, c, own_block(c), local_block(c))
-
-    def core_copy(c):
-        return pltpu.make_async_remote_copy(
-            src_ref=core_s.at[c],
-            dst_ref=core_r.at[c],
-            send_sem=core_ss.at[c],
-            recv_sem=core_rs.at[c],
-            device_id=(sibling, g),
-            device_id_type=MESH,
+
+    def core_copy(c, part_of):
+        return remote(
+            core_s.at[c, part_of], core_r.at[c, part_of], core_ss.at[c], core_rs.at[c], sibling, g
         )
 
     def xin_slab(way):
@@ -385,11 +387,12 @@
         def one(s):
             core_s[c, s] = term(1 - core, c, s)
 
-        loop(GROUP, one)
-        core_copy(c).start()
+        for first in range(0, GROUP, GROUP // 2):
+            loop(GROUP // 2, lambda s: one(first + s))
+            core_copy(c, pl.ds(first, GROUP // 2)).start()
 
     def sum_x(c):
-        core_copy(c).wait_recv()
+        came(core_rs.at[c], core_r.at[c])
 
         def add(s):
             core_r[c, s] = term(core, c, s) + core_r[c, s]
@@ -424,6 +427,10 @@
     def give(rs, t, c, s, member):
         return remote(inc.at[t, c, s], inc.at[t, c, s], give_ss, rs, member, g)
 
+    def give_core(c, owner):
+        pair = inc.at[core, c, pl.ds(2 * owner, 2)]
+        remote(pair, pair, give_ss, ca_rs.at[c], sibling, g).start()
+
     def finish(c):
         y_copy(c).wait_recv()
         for j in range(2):
@@ -432,16 +439,19 @@
         pair = inc.at[core, c, pl.ds(2 * x, 2)]
         for way in range(2):
             remote(pair, pair, give_ss, xa_rs.at[c], x_peer(way), g).start()
+        give_core(c, x)
 
     def gather_x(c):
         came(xa_rs.at[c], inc.at[core, c, pl.ds(0, 4)])
         for way in range(2):
             slab = 2 * around(x, 1 - way) + way
             give(xf_rs.at[c], core, c, slab, x_peer(way)).start()
+        for way in range(2):
+            give_core(c, around(x, way))
 
     def gather_far(c):
         came(xf_rs.at[c], inc.at[core, c, pl.ds(0, 2)])
-        remote(inc.at[core, c], inc.at[core, c], give_ss, ca_rs.at[c], sibling, g).start()
+        give_core(c, around(x, 0, 2))
 
     def weigh(c):
         def one(s):
@@ -454,11 +464,13 @@
                 total = share if total is None else total + share
             core_s[c, s] = total
 
-        core_copy(c).wait_send()
+        left(core_ss.at[c], core_s.at[c])
         came(ca_rs.at[c], inc.at[1 - core, c])
-        loop(GROUP, one)
+        for peer in peers():
+            one(peer)
+            send(2, c, weighted_block(c), line_block(c), peer)
+        one(g)
         lines[c, g] = core_s[c, g]
-        exchange(2, c, weighted_block(c), line_block(c))
         inc_copy(c).start()
 
     def inc_copy(c):
@@ -566,6 +578,28 @@
         grad_copy(c).wait()
 
 
+def hand_over(grad_in, inc_in, grad_out, inc_out, grad_v, inc_v, in_sem, out_sem):
+    pieces = []
+    for source, held, target in ((inc_in, inc_v, inc_out), (grad_in, grad_v, grad_out)):
+        size = source.shape[0] // PIECES
+        for i in range(PIECES):
+            span = pl.ds(i * size, size)
+            sems = in_sem.at[len(pieces)], out_sem.at[len(pieces)]
+            pieces.append(
+                (
+                    pltpu.make_async_copy(source.at[span], held.at[span], sems[0]),
+                    pltpu.make_async_copy(held.at[span], target.at[span], sems[1]),
+                )
+            )
+    for take, _ in pieces:
+        take.start()
+    for take, put in pieces:
+        take.wait()
+        put.start()
+    for _, put in pieces:
+        put.wait()
+
+
 def on_device(alpha, pert, innov, weight, row_class, col_class, rowf, colf, level):
     any_spec = pl.BlockSpec(memory_space=pl.ANY)
     vmem_spec = pl.BlockSpec(memory_space=pltpu.VMEM)
@@ -631,7 +665,17 @@
             collective_id=0, has_side_effects=True, vmem_limit_bytes=62 * 1024 * 1024
         ),
     )(alpha[0], pert[0], innov, weight, row_class, col_class, rowf, colf, level)
-    return gradient[None], increment
+    shapes = (gradient.shape, (2 * LEVELS, ROWS, NX))
+    gradient, increment = pl.pallas_call(
+        hand_over,
+        out_shape=tuple(jax.ShapeDtypeStruct(shape, BF16) for shape in shapes),
+        in_specs=[any_spec] * 2,
+        out_specs=(any_spec, any_spec),
+        scratch_shapes=[pltpu.VMEM(shape, BF16) for shape in shapes]
+        + [dma((2 * PIECES,)), dma((2 * PIECES,))],
+        compiler_params=pltpu.CompilerParams(vmem_limit_bytes=62 * 1024 * 1024),
+    )(gradient, increment.reshape(shapes[1]))
+    return gradient[None], increment.reshape(2, LEVELS, ROWS, NX)
 
 
 def solution(mesh):

time: 139 us -> 138 us (level)
  local copies, waits for them, and re-layouts: 5.31 us -> 0 us
  Pallas kernels: 133 us -> 137 us
    unnamed x4 -> x0, local copies, waits for them, and re-layouts: 5.31 us -> none
    pallas_call x0 -> x1, Pallas kernels: none -> 5.29 us  [on_device(): pl.pallas_call(hand_over, out_shape=tuple((jax.ShapeDtypeStruct(shape, BF...]
    pallas_call x1, Pallas kernels: 133 us -> 132 us  [on_device(): pl.pallas_call(kernel, out_shape=(jax.ShapeDtypeStruct((LEVELS, ROWS, NX)...]
where the time goes in v2:
time: 138 us
  Pallas kernels  137 us (99%)
    pallas_call x1, Pallas kernels, on_device(): pl.pallas_call(kernel, out_shape=(jax.ShapeDtypeStruct((LEVELS, ROWS, NX)...  132 us
    pallas_call x1, Pallas kernels, on_device(): pl.pallas_call(hand_over, out_shape=tuple((jax.ShapeDtypeStruct(shape, BF...  5.29 us

profile of v2, /device:TPU:1, one launch (start us, length us, event | category | flops | bytes accessed | tf_op | source)
XLA Modules:
  0.0 137.5 jit_solution(17675385188131977627)
XLA Ops:
  0.6 131.6 %shard_map.104 = (bf16[16,64,1024]{2,1,0:T(8,128)(2,1)}, bf16[2,16,64,1024]{3,2,1,0:T(8,128)(2,1)}) custom-call(bf16[16,64,1024]{2,1,0:T(8,128)(2,1)} %bitcast.7, bf16[2,16,64,1024]{3,2,1,0:T(8,128)(2,1)} %bitcast.5, bf16[2,16,64,1024]{3,2,1,0:T(8,128)(2,1)} %innov_h.1, f32[2,16,64]{2,1,0:T(8,128)} %weight_ref.1, s32[16,64]{1,0:T(8,128)} %row_ref.1, ...), custom_call_target="tpu_custom_call" | custom-call | tf_op jit(solution)/shard_map/pallas_call | solution.py:655
  132.3 5.3 %shard_map.105 = (bf16[16,64,1024]{2,1,0:T(8,128)(2,1)}, bf16[32,64,1024]{2,1,0:T(8,128)(2,1)}) custom-call(bf16[16,64,1024]{2,1,0:T(8,128)(2,1)} %get-tuple-element.6.grad_in, bf16[32,64,1024]{2,1,0:T(8,128)(2,1)} %bitcast.6), custom_call_target="tpu_custom_call" | custom-call | tf_op jit(solution)/shard_map/pallas_call | solution.py:669

commit v3 on v2

--- a/solution.py
+++ b/solution.py
@@ -16,7 +16,6 @@
 GROUP = 8
 RING = 4
 CHUNKS = 4
-PIECES = 4
 PART = LEVELS // CHUNKS
 ROWS = 64
 ROW_BITS = 6
@@ -49,11 +48,10 @@
 
 def kernel(
     alpha_h, pert_h, innov_h, weight_ref, row_ref, col_ref, rowf_h, colf_h, level_ref,
-    grad_h, inc_h,
+    gradient, increment,
     alpha_v, pert_v, innov_v, rowf, colf, colt, down, back, row_hot, weight_v, masked,
-    slabs, lines, filtered, turned, local_s, local_r, core_s, core_r, x_in, x_got, y_s, y_r,
-    inc, inc_v,
-    alpha_sem, rowf_sem, load_sem, grad_sem, inc_sem, out_sem, a2a_ss, a2a_rs, core_ss, core_rs,
+    slabs, lines, filtered, local_s, local_r, core_s, core_r, x_in, x_got, y_s, y_r, inc,
+    alpha_sem, rowf_sem, load_sem, out_sem, a2a_ss, a2a_rs, core_ss, core_rs,
     x_ss, xin_rs, xgot_rs, yr_ss, yr_rs, give_ss, xa_rs, xf_rs, ca_rs,
 ):
     m = lax.axis_index("member")
@@ -458,8 +456,8 @@
             total = None
             for t in range(2):
                 block = inc[t, c, s]
-                inc_v[t, part(c), :, lane(s)] = block
                 misfit = weight_v[t, part(c)] * (block - innov_v[t, part(c), :, lane(s)])
+                increment[t, part(c), :, lane(s)] = block
                 share = pert_v[t, part(c), :, lane(s)] * misfit
                 total = share if total is None else total + share
             core_s[c, s] = total
@@ -471,26 +469,17 @@
             send(2, c, weighted_block(c), line_block(c), peer)
         one(g)
         lines[c, g] = core_s[c, g]
-        inc_copy(c).start()
-
-    def inc_copy(c):
-        return pltpu.make_async_copy(
-            inc_v.at[:, part(c)], inc_h.at[:, part(c)], inc_sem.at[c]
-        )
 
     def column_adjoint(c):
         lines_came(2, c)
 
         def keep(s, block):
-            turned[c, s] = block
+            local_s[c, s] = block
 
         level_pass(c, back, lines, keep, lambda chunk: range(chunk, CHUNKS))
-        column_pass(c, turned, colf, True)
+        column_pass(c, local_s, colf, True)
         local_r[c, g] = filtered[c, g]
         exchange(3, c, filtered_block(c), local_block(c))
-
-    def grad_copy(c):
-        return pltpu.make_async_copy(alpha_v.at[part(c)], grad_h.at[part(c)], grad_sem.at[c])
 
     def row_adjoint(c):
         local_came(3, c)
@@ -518,11 +507,10 @@
             )
             total = dot(masked[:, n * CLASSES * TILE :], table)
             alpha = alpha_v[levels(c), :, side].reshape(PAIR * LINES, TILE).astype(F32)
-            alpha_v[levels(c), :, side] = (
+            gradient[levels(c), :, side] = (
                 (alpha + total).astype(BF16).reshape(PAIR * PART, ROWS, TILE)
             )
-        for j in range(PAIR):
-            grad_copy(c + j).start()
+
 
     pl.semaphore_wait(barrier, GROUP + 3)
     for c in range(1, CHUNKS):
@@ -562,42 +550,19 @@
 
     loop(CHUNKS + 7, forward)
 
+    exchange_left(1)
+
     def backward(step):
         at(step, 0, lambda c: column_adjoint(CHUNKS - 1 - c))
         at(step, 2, lambda c: row_adjoint(CHUNKS - 1 - c))
 
     loop(CHUNKS + 2, backward)
 
-    for phase in range(4):
+    for phase in (0, 2, 3):
         exchange_left(phase)
     left(x_ss, core_r.at[pl.ds(0, 3)])
     left(yr_ss, y_s)
     left(give_ss, pert_v.at[:, pl.ds(0, LEVELS - 2)])
-    for c in range(CHUNKS):
-        inc_copy(c).wait()
-        grad_copy(c).wait()
-
-
-def hand_over(grad_in, inc_in, grad_out, inc_out, grad_v, inc_v, in_sem, out_sem):
-    pieces = []
-    for source, held, target in ((inc_in, inc_v, inc_out), (grad_in, grad_v, grad_out)):
-        size = source.shape[0] // PIECES
-        for i in range(PIECES):
-            span = pl.ds(i * size, size)
-            sems = in_sem.at[len(pieces)], out_sem.at[len(pieces)]
-            pieces.append(
-                (
-                    pltpu.make_async_copy(source.at[span], held.at[span], sems[0]),
-                    pltpu.make_async_copy(held.at[span], target.at[span], sems[1]),
-                )
-            )
-    for take, _ in pieces:
-        take.start()
-    for take, put in pieces:
-        take.wait()
-        put.start()
-    for _, put in pieces:
-        put.wait()
 
 
 def on_device(alpha, pert, innov, weight, row_class, col_class, rowf, colf, level):
@@ -625,18 +590,14 @@
         pltpu.VMEM(slab, BF16),
         pltpu.VMEM(slab, BF16),
         pltpu.VMEM(slab, BF16),
-        pltpu.VMEM(slab, BF16),
         pltpu.VMEM((CHUNKS, 2) + block, BF16),
         pltpu.VMEM((CHUNKS, 2, 2) + block, BF16),
         pltpu.VMEM((CHUNKS, 2) + block, BF16),
         pltpu.VMEM((CHUNKS, 2) + block, BF16),
         pltpu.VMEM((2,) + slab, BF16),
-        pltpu.VMEM((2, LEVELS, ROWS, NX), BF16),
         dma((CHUNKS,)),
         dma((NX // TILE,)),
         dma((3,)),
-        dma((CHUNKS,)),
-        dma((CHUNKS,)),
         dma,
         dma((4,)),
         dma((4, CHUNKS)),
@@ -655,27 +616,17 @@
     gradient, increment = pl.pallas_call(
         kernel,
         out_shape=(
-            jax.ShapeDtypeStruct((LEVELS, ROWS, NX), BF16),
-            jax.ShapeDtypeStruct((2, LEVELS, ROWS, NX), BF16),
+            pltpu.VMEM((LEVELS, ROWS, NX), BF16),
+            pltpu.VMEM((2, LEVELS, ROWS, NX), BF16),
         ),
         in_specs=[any_spec] * 3 + [vmem_spec] * 3 + [any_spec] * 2 + [vmem_spec],
-        out_specs=(any_spec, any_spec),
+        out_specs=(vmem_spec, vmem_spec),
         scratch_shapes=scratch,
         compiler_params=pltpu.CompilerParams(
-            collective_id=0, has_side_effects=True, vmem_limit_bytes=62 * 1024 * 1024
+            collective_id=0, has_side_effects=True, vmem_limit_bytes=56 * 1024 * 1024
         ),
     )(alpha[0], pert[0], innov, weight, row_class, col_class, rowf, colf, level)
-    shapes = (gradient.shape, (2 * LEVELS, ROWS, NX))
-    gradient, increment = pl.pallas_call(
-        hand_over,
-        out_shape=tuple(jax.ShapeDtypeStruct(shape, BF16) for shape in shapes),
-        in_specs=[any_spec] * 2,
-        out_specs=(any_spec, any_spec),
-        scratch_shapes=[pltpu.VMEM(shape, BF16) for shape in shapes]
-        + [dma((2 * PIECES,)), dma((2 * PIECES,))],
-        compiler_params=pltpu.CompilerParams(vmem_limit_bytes=62 * 1024 * 1024),
-    )(gradient, increment.reshape(shapes[1]))
-    return gradient[None], increment.reshape(2, LEVELS, ROWS, NX)
+    return gradient[None], increment
 
 
 def solution(mesh):

time: 138 us -> 135 us (0.978)
  Pallas kernels: 137 us -> 131 us
  local copies, waits for them, and re-layouts: 0 us -> 3.33 us
    pallas_call x2 -> x1, Pallas kernels: 137 us -> 131 us  [on_device(): pl.pallas_call(kernel, out_shape=(pltpu.VMEM((LEVELS, ROWS, NX), BF16), p...]
    unnamed x0 -> x2, local copies, waits for them, and re-layouts: none -> 3.33 us
where the time goes in v3:
time: 135 us
  Pallas kernels  131 us (97%)
  local copies, waits for them, and re-layouts  3.33 us (2%)
    pallas_call x1, Pallas kernels, on_device(): pl.pallas_call(kernel, out_shape=(pltpu.VMEM((LEVELS, ROWS, NX), BF16), p...  131 us
    unnamed x2, local copies, waits for them, and re-layouts  3.33 us

profile of v3, /device:TPU:1, one launch (start us, length us, event | category | flops | bytes accessed | tf_op | source)
XLA Modules:
  0.0 134.7 jit_solution(3180341946603393378)
XLA Ops:
  0.6 130.7 %shard_map.104 = (bf16[16,64,1024]{2,1,0:T(8,128)(2,1)S(1)}, bf16[2,16,64,1024]{3,2,1,0:T(8,128)(2,1)S(1)}) custom-call(bf16[16,64,1024]{2,1,0:T(8,128)(2,1)} %bitcast.5, bf16[2,16,64,1024]{3,2,1,0:T(8,128)(2,1)} %bitcast.4, bf16[2,16,64,1024]{3,2,1,0:T(8,128)(2,1)} %innov_h.1, f32[2,16,64]{2,1,0:T(8,128)} %weight_ref.1, s32[16,64]{1,0:T(8,128)} %row_ref.1, ...), custom_call_target="tpu_custom_call" | custom-call | tf_op jit(solution)/shard_map/pallas_call | solution.py:616
  131.3 1.3 copy.13
  132.7 2.0 %copy.14 = bf16[2,16,64,1024]{3,2,1,0:T(8,128)(2,1)} copy(bf16[2,16,64,1024]{3,2,1,0:T(8,128)(2,1)S(1)} %get-tuple-element.7) | data formatting | bytes 8388608

commit v4 on v3

--- a/solution.py
+++ b/solution.py
@@ -532,23 +532,23 @@
         def _():
             adjoint_tables()
 
-        at(step, 4, sum_core)
+        at(step, 4, sum_x)
+
+        @pl.when(step == 2)
+        def _():
+            column_tables()
+
+        at(step, 2, column_filter)
+        at(step, 7, gather_x)
         at(step, 6, finish)
+        at(step, 8, weigh)
+        at(step, 3, sum_core)
+        at(step, 5, sum_y)
         at(step, 7, gather_far)
-        at(step, 5, sum_y)
-        at(step, 1, row_filter)
-        at(step, 4, sum_x)
-        at(step, 7, weigh)
-
-        @pl.when(step == 2)
-        def _():
-            column_tables()
-
-        at(step, 2, column_filter)
-        at(step, 6, gather_x)
         at(step, 4, add_x)
-
-    loop(CHUNKS + 7, forward)
+        at(step, 0, row_filter)
+
+    loop(CHUNKS + 8, forward)
 
     exchange_left(1)
 

time: 135 us -> 139 us (1.030)
  Pallas kernels: 131 us -> 134 us
    pallas_call x1, Pallas kernels: 131 us -> 134 us  [on_device(): pl.pallas_call(kernel, out_shape=(pltpu.VMEM((LEVELS, ROWS, NX), BF16), p...]
where the time goes in v4:
time: 139 us; the launch traced here: 138 us
  Pallas kernels  134 us (96%)
  local copies, waits for them, and re-layouts  3.33 us (2%)
    pallas_call x1, Pallas kernels, on_device(): pl.pallas_call(kernel, out_shape=(pltpu.VMEM((LEVELS, ROWS, NX), BF16), p...  134 us
    unnamed x2, local copies, waits for them, and re-layouts  3.33 us

profile of v4, /device:TPU:1, one launch (start us, length us, event | category | flops | bytes accessed | tf_op | source)
XLA Modules:
  0.0 137.8 jit_solution(11976532974951583004)
XLA Ops:
  0.6 133.9 %shard_map.104 = (bf16[16,64,1024]{2,1,0:T(8,128)(2,1)S(1)}, bf16[2,16,64,1024]{3,2,1,0:T(8,128)(2,1)S(1)}) custom-call(bf16[16,64,1024]{2,1,0:T(8,128)(2,1)} %bitcast.5, bf16[2,16,64,1024]{3,2,1,0:T(8,128)(2,1)} %bitcast.4, bf16[2,16,64,1024]{3,2,1,0:T(8,128)(2,1)} %innov_h.1, f32[2,16,64]{2,1,0:T(8,128)} %weight_ref.1, s32[16,64]{1,0:T(8,128)} %row_ref.1, ...), custom_call_target="tpu_custom_call" | custom-call | tf_op jit(solution)/shard_map/pallas_call | solution.py:616
  134.5 1.3 copy.13
  135.8 2.0 %copy.14 = bf16[2,16,64,1024]{3,2,1,0:T(8,128)(2,1)} copy(bf16[2,16,64,1024]{3,2,1,0:T(8,128)(2,1)S(1)} %get-tuple-element.7) | data formatting | bytes 8388608

commit v5 on v3

--- a/solution.py
+++ b/solution.py
@@ -23,7 +23,7 @@
 NX = GROUP * LANES
 NY = GROUP * ROWS
 LINES = PART * ROWS
-PAIR = 2
+PAIR = 1
 TILE = 256
 TILES = NX // TILE
 WIDE = 2

time: 135 us -> 131 us (0.970)
  Pallas kernels: 131 us -> 127 us
    pallas_call x1, Pallas kernels: 131 us -> 127 us  [on_device(): pl.pallas_call(kernel, out_shape=(pltpu.VMEM((LEVELS, ROWS, NX), BF16), p...]
where the time goes in v5:
time: 131 us
  Pallas kernels  127 us (97%)
  local copies, waits for them, and re-layouts  3.33 us (3%)
    pallas_call x1, Pallas kernels, on_device(): pl.pallas_call(kernel, out_shape=(pltpu.VMEM((LEVELS, ROWS, NX), BF16), p...  127 us
    unnamed x2, local copies, waits for them, and re-layouts  3.33 us

profile of v5, /device:TPU:1, one launch (start us, length us, event | category | flops | bytes accessed | tf_op | source)
XLA Modules:
  0.0 131.3 jit_solution(16835268293354669829)
XLA Ops:
  0.6 127.3 %shard_map.104 = (bf16[16,64,1024]{2,1,0:T(8,128)(2,1)S(1)}, bf16[2,16,64,1024]{3,2,1,0:T(8,128)(2,1)S(1)}) custom-call(bf16[16,64,1024]{2,1,0:T(8,128)(2,1)} %bitcast.5, bf16[2,16,64,1024]{3,2,1,0:T(8,128)(2,1)} %bitcast.4, bf16[2,16,64,1024]{3,2,1,0:T(8,128)(2,1)} %innov_h.1, f32[2,16,64]{2,1,0:T(8,128)} %weight_ref.1, s32[16,64]{1,0:T(8,128)} %row_ref.1, ...), custom_call_target="tpu_custom_call" | custom-call | tf_op jit(solution)/shard_map/pallas_call | solution.py:616
  128.0 1.3 %copy.13 = bf16[1,16,64,1024]{3,2,1,0:T(8,128)(2,1)} copy(bf16[1,16,64,1024]{3,2,1,0:T(8,128)(2,1)S(1)} %bitcast.3) | data formatting | bytes 4194304
  129.3 2.0 %copy.14 = bf16[2,16,64,1024]{3,2,1,0:T(8,128)(2,1)} copy(bf16[2,16,64,1024]{3,2,1,0:T(8,128)(2,1)S(1)} %get-tuple-element.7) | data formatting | bytes 8388608
